TPU v7x, 128 devices: a whole 4x4x4 slice. The times are simulated.
128 devices in a mesh: dp: 8 (over x_lo, z), tensor: 16 (over x_hi, y, core).
Axes of the slice: x: 4 (x_hi: 2, x_lo: 2; x = x_hi * 2 + x_lo), y: 4, z: 4, core: 2. Of those that a mesh axis runs over, the one named last changes fastest.
Arguments:
- tokens: bfloat16 [8, 2048, 4096], P('dp', 'tensor'), may hold values from -1.8 to 1.8
- cotangent: bfloat16 [8, 2048, 4096], P('dp', None, 'tensor'), may hold values from -6 to 6
- gain: float32 [4096], replicated, may hold values from 0.25 to 3.5
- w_query: bfloat16 [4096, 4096], P(None, 'tensor'), may hold values from -6 to 6
- w_key: bfloat16 [4096, 512], P(None, 'tensor'), may hold values from -6 to 6
- w_value: bfloat16 [4096, 512], P(None, 'tensor'), may hold values from -6 to 6
- moment_query: float32 [4096, 4096], P('dp', 'tensor'), may hold values from -6 to 6
- moment_key: float32 [4096, 512], P('dp', 'tensor'), may hold values from -6 to 6
- moment_value: float32 [4096, 512], P('dp', 'tensor'), may hold values from -6 to 6
Outputs:
- attended: bfloat16 [8, 2048, 4096], P('dp', None, 'tensor')
- grad_tokens: bfloat16 [8, 2048, 4096], P('dp', 'tensor')
- fresh_query: bfloat16 [4096, 4096], P(None, 'tensor')
- fresh_key: bfloat16 [4096, 512], P(None, 'tensor')
- fresh_value: bfloat16 [4096, 512], P(None, 'tensor')
- next_query: float32 [4096, 4096], P('dp', 'tensor')
- next_key: float32 [4096, 512], P('dp', 'tensor')
- next_value: float32 [4096, 512], P('dp', 'tensor')
All inputs are finite; a program needn't handle non-finite values.
Results may differ from a plain program's by a relative error of at most 0.017.
Values may be sent and summed in bfloat16 or wider, within the bound.
A program may use at most 256 MiB of HBM per device.

v0:
```python
import jax
import jax.numpy as jnp
from jax import lax
from jax.sharding import Mesh
from jax.sharding import PartitionSpec as P

D = 4096
HEADS = 32
KVH = 4
HD = 128
TENSOR = ("tensor_0", "tensor_1", "tensor_2")
DP = ("dp_0", "dp_1")
DP_TENSOR = ("dp_0", "dp_1", "tensor_0", "tensor_1", "tensor_2")
rope_base = 1000000.0
norm_eps = 1e-06
stat_eps = 1e-06
learn_rate = 0.05
keep_rate = 0.9


def partner_2(shard, axis, distance):
    return lax.ppermute(shard, axis, [(i, i ^ 1 << distance) for i in range(lax.axis_size(axis))])


def in_blocks(shard, dim, size):
    lengths = shard.shape
    pieces = shard.reshape(*lengths[:dim], size, lengths[dim] // size, *lengths[dim + 1 :])
    return jnp.moveaxis(pieces, dim, 0)


def summed_rows(shard, chips, core, dim):
    sizes = (lax.axis_size(chips), lax.axis_size(core))
    pieces = in_blocks(shard, dim, sizes[0] * sizes[1])
    inside = pieces.shape[1:]
    pieces = pieces.reshape(*sizes, *inside).swapaxes(0, 1).reshape(-1, *inside)
    pieces = lax.psum_scatter(pieces, core, scatter_dimension=0, tiled=True)
    return lax.psum_scatter(pieces, chips, scatter_dimension=0, tiled=True)[0]


def side_by_side(arrays, axis, dim, along):
    both = jnp.concatenate(arrays, axis=along)
    out, at, done = (lax.psum_scatter(both, axis, scatter_dimension=dim, tiled=True), 0, [])
    for a in arrays:
        done.append(lax.slice_in_dim(out, at, at + a.shape[along], axis=along))
        at += a.shape[along]
    return tuple(done)


def one_axis_at_a_time(shard, axes):
    for axis in axes:
        shard = lax.psum(shard, axis)
    return shard


def in_one_piece(arrays, axis, dim, along):
    ends, at = ([], 0)
    for a in arrays[:-1]:
        at += a.shape[along]
        ends.append(at)
    both = jnp.concatenate(arrays, axis=along)
    return tuple(jnp.split(lax.all_gather(both, axis, axis=dim, tiled=True), ends, axis=along))


def rotate(matrix, first_column, head_size, sign):
    length = matrix.shape[0]
    columns = matrix.shape[1]
    index = first_column + jnp.arange(columns, dtype=jnp.int32)
    within = index % head_size // 2
    rates = jnp.power(jnp.float32(rope_base), within.astype(jnp.float32) * (-2.0 / head_size))
    angle = jnp.arange(length, dtype=jnp.float32)[:, None] * rates[None, :]
    even = index % 2 == 0
    partner = jnp.where(even[None, :], -jnp.roll(matrix, -1, axis=1), jnp.roll(matrix, 1, axis=1))
    return matrix * jnp.cos(angle) + partner * (sign * jnp.sin(angle))


def per_device(
    tokens, cotangent, gain, w_query, w_key, w_value, moment_query, moment_key, moment_value
):
    rank = lax.axis_index(TENSOR)
    query_width = w_query.shape[1]
    key_width = w_key.shape[1]
    local_heads = query_width // HD
    width = tokens.shape[2]
    in_scale = width ** (-0.5)
    head_scale = HD ** (-0.5)
    inputs = tokens[0].astype(jnp.float32)
    reciprocal = lax.rsqrt(jnp.mean(inputs * inputs, axis=1, keepdims=True) + norm_eps)
    unit_rows = inputs * reciprocal
    normed = (unit_rows * gain).astype(jnp.bfloat16)
    normed_all = lax.all_gather(normed, TENSOR, axis=0, tiled=True)
    length = normed_all.shape[0]
    query = rotate(
        jnp.dot(normed_all, w_query, preferred_element_type=jnp.float32) * in_scale,
        rank * query_width,
        HD,
        1.0,
    ).astype(jnp.bfloat16)
    key_part = rotate(
        jnp.dot(normed_all, w_key, preferred_element_type=jnp.float32) * in_scale,
        rank * key_width,
        HD,
        1.0,
    ).astype(jnp.bfloat16)
    value_part = (
        jnp.dot(normed_all, w_value, preferred_element_type=jnp.float32) * in_scale
    ).astype(jnp.bfloat16)
    span = lax.axis_size(TENSOR) // KVH
    levels = span.bit_length() - 1
    paired = jnp.stack([key_part, value_part])
    for level in range(levels):
        other = partner_2(paired, TENSOR, level)
        higher = rank // 2**level % 2 == 1
        paired = jnp.where(
            higher,
            jnp.concatenate([other, paired], axis=2),
            jnp.concatenate([paired, other], axis=2),
        )
    key_head = paired[0]
    value_head = paired[1]
    query_heads = query.reshape(length, local_heads, HD)
    grad_heads = cotangent[0].reshape(length, local_heads, HD)
    rows_block = 512
    starts = jnp.arange(length // rows_block, dtype=jnp.int32) * rows_block
    places = jnp.arange(length)

    def attend(carry, start):
        query_rows = lax.dynamic_slice_in_dim(query_heads, start, rows_block, 0)
        grad_rows = lax.dynamic_slice_in_dim(grad_heads, start, rows_block, 0)
        scores = (
            jnp.einsum("shd,td->hst", query_rows, key_head, preferred_element_type=jnp.float32)
            * head_scale
        )
        row_places = start + jnp.arange(rows_block)
        causal = row_places[:, None] >= places[None, :]
        attention = jax.nn.softmax(jnp.where(causal[None], scores, -1e30), axis=2)
        attention_low = attention.astype(jnp.bfloat16)
        attended_rows = jnp.einsum(
            "hst,td->shd", attention_low, value_head, preferred_element_type=jnp.float32
        ).astype(jnp.bfloat16)
        grad_raw = jnp.einsum(
            "shd,td->hst", grad_rows, value_head, preferred_element_type=jnp.float32
        )
        grad_scores = attention * (grad_raw - jnp.sum(attention * grad_raw, axis=2, keepdims=True))
        grad_low = (grad_scores * head_scale).astype(jnp.bfloat16)
        query_grad_rows = jnp.einsum(
            "hst,td->shd", grad_low, key_head, preferred_element_type=jnp.float32
        )
        key_term = jnp.einsum(
            "hst,shd->td", grad_low, query_rows, preferred_element_type=jnp.float32
        )
        value_term = jnp.einsum(
            "hst,shd->td", attention_low, grad_rows, preferred_element_type=jnp.float32
        )
        return ((carry[0] + key_term, carry[1] + value_term), (attended_rows, query_grad_rows))

    empty = jnp.zeros((length, HD), jnp.float32)
    (key_local, value_local), (attended_blocks, query_blocks) = lax.scan(
        attend, (empty, empty), starts
    )
    attended = attended_blocks.reshape(length, query_width)
    grad_query_raw = query_blocks.reshape(length, query_width)
    current = lax.optimization_barrier(
        jnp.stack([key_local, value_local]).astype(jnp.bfloat16)
    ).astype(jnp.float32)
    for level in reversed(range(levels)):
        middle = current.shape[2] // 2
        higher = rank // 2**level % 2 == 1
        outgoing = jnp.where(higher, current[:, :, :middle], current[:, :, middle:])
        retained = jnp.where(higher, current[:, :, middle:], current[:, :, :middle])
        current = retained + partner_2(outgoing.astype(jnp.bfloat16), TENSOR, level).astype(
            outgoing.dtype
        )
    grad_key = rotate(current[0], rank * key_width, HD, -1.0).astype(jnp.bfloat16)
    grad_value = current[1].astype(jnp.bfloat16)
    grad_query = rotate(grad_query_raw, rank * query_width, HD, -1.0).astype(jnp.bfloat16)

    def product(grad, weight):
        return jnp.einsum("sc,dc->sd", grad, weight, preferred_element_type=jnp.float32)

    grad_normed = summed_rows(
        (
            (product(grad_query, w_query) + product(grad_key, w_key) + product(grad_value, w_value))
            * in_scale
        ).astype(jnp.bfloat16),
        ("tensor_0", "tensor_1"),
        "tensor_2",
        0,
    ).astype(jnp.float32)
    grad_unit = grad_normed * gain
    inner = jnp.mean(grad_unit * unit_rows, axis=1, keepdims=True)
    grad_tokens = (reciprocal * (grad_unit - unit_rows * inner)).astype(jnp.bfloat16)[None]
    grad_wq = (
        jnp.einsum("sd,sc->dc", normed_all, grad_query, preferred_element_type=jnp.float32)
        * in_scale
    )
    grad_wk = (
        jnp.einsum("sd,sc->dc", normed_all, grad_key, preferred_element_type=jnp.float32) * in_scale
    )
    grad_wv = (
        jnp.einsum("sd,sc->dc", normed_all, grad_value, preferred_element_type=jnp.float32)
        * in_scale
    )
    summed_query, summed_key, summed_value = tuple(
        (
            part.astype(jnp.float32)
            for part in side_by_side(
                (
                    grad_wq.astype(jnp.bfloat16),
                    grad_wk.astype(jnp.bfloat16),
                    grad_wv.astype(jnp.bfloat16),
                ),
                DP,
                0,
                1,
            )
        )
    )
    square = (
        jnp.sum(summed_query * summed_query)
        + jnp.sum(summed_key * summed_key)
        + jnp.sum(summed_value * summed_value)
    )
    total = one_axis_at_a_time(square, DP_TENSOR)
    count_all = 1.0 * D * HD * (HEADS + 2 * KVH)
    factor = lax.rsqrt(total / count_all + stat_eps)
    dp_rank = lax.axis_index(DP)

    def advance(weight_own, moment, summed):
        moved = keep_rate * moment + summed * factor
        return ((weight_own.astype(jnp.float32) - learn_rate * moved).astype(jnp.bfloat16), moved)

    share = moment_query.shape[0]
    own_query = lax.dynamic_slice_in_dim(w_query, dp_rank * share, share, 0)
    own_key = lax.dynamic_slice_in_dim(w_key, dp_rank * share, share, 0)
    own_value = lax.dynamic_slice_in_dim(w_value, dp_rank * share, share, 0)
    part_query, next_query = advance(own_query, moment_query, summed_query)
    part_key, next_key = advance(own_key, moment_key, summed_key)
    part_value, next_value = advance(own_value, moment_value, summed_value)
    fresh_query, fresh_key, fresh_value = in_one_piece((part_query, part_key, part_value), DP, 0, 1)
    return (
        attended[None],
        grad_tokens,
        fresh_query,
        fresh_key,
        fresh_value,
        next_query,
        next_key,
        next_value,
    )


def solution(mesh):
    torus = Mesh(
        mesh.devices.reshape(2, 4, 2, 4, 2), ("dp_0", "dp_1", "tensor_0", "tensor_1", "tensor_2")
    )
    placed = (
        P(DP, TENSOR, None),
        P(DP, None, TENSOR),
        P(),
        P(None, TENSOR),
        P(None, TENSOR),
        P(None, TENSOR),
        P(DP, TENSOR),
        P(DP, TENSOR),
        P(DP, TENSOR),
    )
    return jax.shard_map(
        per_device,
        mesh=torus,
        in_specs=placed,
        out_specs=(
            P(DP, None, TENSOR),
            P(DP, TENSOR, None),
            P(None, TENSOR),
            P(None, TENSOR),
            P(None, TENSOR),
            P(DP, TENSOR),
            P(DP, TENSOR),
            P(DP, TENSOR),
        ),
        check_vma=False,
    )
```

profile of v0, /device:TPU:1, one launch (start us, length us, event | category | flops | bytes accessed | tf_op | source)
XLA Modules:
  0.0 772.4 jit_solution(11540395952958526187)
XLA Ops:
  13.9 111.1 %all-gather.3.cloned.1.call-done = bf16[2048,4096]{1,0:T(8,128)(2,1)} async-done(((bf16[128,4096]{1,0:T(8,128)(2,1)}), bf16[2048,4096]{1,0:T(8,128)(2,1)}) %all-gather.3.cloned.1.call-update) | async-done | bytes 16777232 | tf_op jit(solution)/shard_map/all_gather | solution.py:90
  125.0 10.9 %convolution_multiply_fusion.5 = f32[2048,32]{0,1:T(8,128)S(1)} fusion(bf16[2048,4096]{1,0:T(8,128)(2,1)} %all-gather.3.cloned.1.call-done, bf16[4096,32]{0,1:T(8,128)(2,1)S(1)} %copy-done.11), kind=kOutput, calls=%fused_computation.75 | convolution fusion | flops 536936448 | bytes 17301504 | tf_op jit(solution)/shard_map/dot_general | solution.py:99
  143.0 9.7 %convolution_multiply_fusion.3 = f32[2048,256]{0,1:T(8,128)} fusion(bf16[2048,4096]{1,0:T(8,128)(2,1)} %all-gather.3.cloned.1.call-done, bf16[4096,256]{1,0:T(8,128)(2,1)S(1)} %copy-done), kind=kOutput, calls=%fused_computation.64 | convolution fusion | flops 4295491584 | bytes 20971520 | tf_op jit(solution)/shard_map/dot_general | solution.py:93
  155.9 10.3 %fusion.83 = bf16[2048,256]{0,1:T(8,128)(2,1)} fusion(f32[2048,1]{0,1:T(1,128)S(1)} %get-tuple-element.180, f32[2048,255]{0,1:T(8,128)S(1)} %get-tuple-element.182, f32[2048,255]{0,1:T(8,128)S(1)} %get-tuple-element.181, f32[2048,1]{0,1:T(1,128)S(1)} %get-tuple-element.179, f32[2048,256]{0,1:T(8,128)S(1)} %copy-done.4, f32[256]{0:T(256)S(1)} %multiply_power_fusion, ...), kind=kLoop, calls=%fused_computation.90 | loop fusion | flops 4718592 | bytes 7341312 | tf_op jit(solution)/shard_map/convert_element_type | solution.py:97
  171.4 280.0 %while.17 = (s32[]{:T(128)}, f32[2048,128]{1,0:T(8,128)}, f32[2048,128]{1,0:T(8,128)}, bf16[4,512,2,128]{3,2,1,0:T(2,128)(2,1)}, f32[4,512,2,128]{1,0,3,2:T(4,12...) while((s32[]{:T(128)}, f32[2048,128]{1,0:T(8,128)}, ...), condition=%wide.region_5.6_spmd.clone, body=%wide.region_1.5_spmd.clone.sunk | while | flops 3269599744 | bytes 147091824 | solution.py:157
  175.3 8.0 %fusion.179 = (f32[2,512]{1,0:T(2,128)S(1)}, f32[2,512,2048]{2,1,0:T(8,128)}) fusion(pred[512,2048]{1,0:T(8,128)(4,1)S(1)} %iota_compare_fusion.2, bf16[2048,128]{1,0:T(8,128)(2,1)} %get-tuple-element.293, bf16[2048,2,128]{0,2,1:T(8,128)(2,1)} %get-tuple-element.292, s32[]{:T(128)S(6)} %select_n.260), kind=kOutput, calls=%fused_computation.174.clone.1 | convolution fusion | flops 545261568 | bytes 10227716 | tf_op jit(solution)/shard_map/while/body/eval_jaxpr/sub | solution.py:135
  197.7 12.8 %fusion.183 = f32[1,512,2,128]{3,1,2,0:T(8,128)S(1)} fusion(f32[512,2,2048]{2,0,1:T(8,128)} %fusion.178, bf16[2048,128]{1,0:T(8,128)(2,1)S(1)} %copy-done.18, f32[2,512,2048]{2,1,0:T(8,128)} %get-tuple-element.258, f32[2,512]{1,0:T(2,128)S(1)} %get-tuple-element.259), kind=kOutput, calls=%fused_computation.28.clone.1 | convolution fusion | flops 551554048 | bytes 17829888 | tf_op jit(solution)/shard_map/while/body/eval_jaxpr/hst,td->shd/dot_general | solution.py:145
  210.5 19.4 %fusion.180 = f32[2048,128]{1,0:T(8,128)} fusion(f32[512,2,2048]{2,0,1:T(8,128)} %fusion.178, f32[2048,128]{1,0:T(8,128)} %get-tuple-element.274, pred[]{:T(512)S(6)} %compare.38, bf16[2048,2,128]{0,2,1:T(8,128)(2,1)} %get-tuple-element.292, s32[]{:T(128)S(6)} %select_n.260, f32[2,512,2048]{2,1,0:T(8,128)} %get-tuple-element.258, ...), kind=kOutput, calls=%fused_computation.24.clone.1 | convolution fusion | flops 552078336 | bytes 35921924 | tf_op jit(solution)/shard_map/while/body/eval_jaxpr/hst,shd->td/dot_general | solution.py:148
  230.3 11.1 %dynamic_update_slice.14 = f32[4,512,2,128]{1,0,3,2:T(4,128)} dynamic-update-slice(f32[4,512,2,128]{1,0,3,2:T(4,128)} %get-tuple-element.277, f32[1,512,2,128]{1,0,3,2:T(1,128)S(1)} %copy.66, s32[]{:T(128)S(6)} %copy.74, s32[]{:T(128)} %constant.177.clone.1..sunk, s32[]{:T(128)} %constant.177.clone.1..sunk, s32[]{:T(128)} %constant.177.clone.1..sunk) | dynamic-update-slice | bytes 1048580 | tf_op jit(solution)/shard_map/while/body/jit(dynamic_update_index_in_dim)/dynamic_update_slice | solution.py:157
  245.2 8.0 %fusion.179 = (f32[2,512]{1,0:T(2,128)S(1)}, f32[2,512,2048]{2,1,0:T(8,128)}) fusion(pred[512,2048]{1,0:T(8,128)(4,1)S(1)} %iota_compare_fusion.2, bf16[2048,128]{1,0:T(8,128)(2,1)} %get-tuple-element.293, bf16[2048,2,128]{0,2,1:T(8,128)(2,1)} %get-tuple-element.292, s32[]{:T(128)S(6)} %select_n.260), kind=kOutput, calls=%fused_computation.174.clone.1 | convolution fusion | flops 545261568 | bytes 10227716 | tf_op jit(solution)/shard_map/while/body/eval_jaxpr/sub | solution.py:135
  267.6 12.8 %fusion.183 = f32[1,512,2,128]{3,1,2,0:T(8,128)S(1)} fusion(f32[512,2,2048]{2,0,1:T(8,128)} %fusion.178, bf16[2048,128]{1,0:T(8,128)(2,1)S(1)} %copy-done.18, f32[2,512,2048]{2,1,0:T(8,128)} %get-tuple-element.258, f32[2,512]{1,0:T(2,128)S(1)} %get-tuple-element.259), kind=kOutput, calls=%fused_computation.28.clone.1 | convolution fusion | flops 551554048 | bytes 17829888 | tf_op jit(solution)/shard_map/while/body/eval_jaxpr/hst,td->shd/dot_general | solution.py:145
  280.4 19.4 %fusion.180 = f32[2048,128]{1,0:T(8,128)} fusion(f32[512,2,2048]{2,0,1:T(8,128)} %fusion.178, f32[2048,128]{1,0:T(8,128)} %get-tuple-element.274, pred[]{:T(512)S(6)} %compare.38, bf16[2048,2,128]{0,2,1:T(8,128)(2,1)} %get-tuple-element.292, s32[]{:T(128)S(6)} %select_n.260, f32[2,512,2048]{2,1,0:T(8,128)} %get-tuple-element.258, ...), kind=kOutput, calls=%fused_computation.24.clone.1 | convolution fusion | flops 552078336 | bytes 35921924 | tf_op jit(solution)/shard_map/while/body/eval_jaxpr/hst,shd->td/dot_general | solution.py:148
  300.2 11.1 %dynamic_update_slice.14 = f32[4,512,2,128]{1,0,3,2:T(4,128)} dynamic-update-slice(f32[4,512,2,128]{1,0,3,2:T(4,128)} %get-tuple-element.277, f32[1,512,2,128]{1,0,3,2:T(1,128)S(1)} %copy.66, s32[]{:T(128)S(6)} %copy.74, s32[]{:T(128)} %constant.177.clone.1..sunk, s32[]{:T(128)} %constant.177.clone.1..sunk, s32[]{:T(128)} %constant.177.clone.1..sunk) | dynamic-update-slice | bytes 1048580 | tf_op jit(solution)/shard_map/while/body/jit(dynamic_update_index_in_dim)/dynamic_update_slice | solution.py:157
  315.1 8.0 %fusion.179 = (f32[2,512]{1,0:T(2,128)S(1)}, f32[2,512,2048]{2,1,0:T(8,128)}) fusion(pred[512,2048]{1,0:T(8,128)(4,1)S(1)} %iota_compare_fusion.2, bf16[2048,128]{1,0:T(8,128)(2,1)} %get-tuple-element.293, bf16[2048,2,128]{0,2,1:T(8,128)(2,1)} %get-tuple-element.292, s32[]{:T(128)S(6)} %select_n.260), kind=kOutput, calls=%fused_computation.174.clone.1 | convolution fusion | flops 545261568 | bytes 10227716 | tf_op jit(solution)/shard_map/while/body/eval_jaxpr/sub | solution.py:135
  337.5 12.8 %fusion.183 = f32[1,512,2,128]{3,1,2,0:T(8,128)S(1)} fusion(f32[512,2,2048]{2,0,1:T(8,128)} %fusion.178, bf16[2048,128]{1,0:T(8,128)(2,1)S(1)} %copy-done.18, f32[2,512,2048]{2,1,0:T(8,128)} %get-tuple-element.258, f32[2,512]{1,0:T(2,128)S(1)} %get-tuple-element.259), kind=kOutput, calls=%fused_computation.28.clone.1 | convolution fusion | flops 551554048 | bytes 17829888 | tf_op jit(solution)/shard_map/while/body/eval_jaxpr/hst,td->shd/dot_general | solution.py:145
  350.3 19.4 %fusion.180 = f32[2048,128]{1,0:T(8,128)} fusion(f32[512,2,2048]{2,0,1:T(8,128)} %fusion.178, f32[2048,128]{1,0:T(8,128)} %get-tuple-element.274, pred[]{:T(512)S(6)} %compare.38, bf16[2048,2,128]{0,2,1:T(8,128)(2,1)} %get-tuple-element.292, s32[]{:T(128)S(6)} %select_n.260, f32[2,512,2048]{2,1,0:T(8,128)} %get-tuple-element.258, ...), kind=kOutput, calls=%fused_computation.24.clone.1 | convolution fusion | flops 552078336 | bytes 35921924 | tf_op jit(solution)/shard_map/while/body/eval_jaxpr/hst,shd->td/dot_general | solution.py:148
  370.1 11.1 %dynamic_update_slice.14 = f32[4,512,2,128]{1,0,3,2:T(4,128)} dynamic-update-slice(f32[4,512,2,128]{1,0,3,2:T(4,128)} %get-tuple-element.277, f32[1,512,2,128]{1,0,3,2:T(1,128)S(1)} %copy.66, s32[]{:T(128)S(6)} %copy.74, s32[]{:T(128)} %constant.177.clone.1..sunk, s32[]{:T(128)} %constant.177.clone.1..sunk, s32[]{:T(128)} %constant.177.clone.1..sunk) | dynamic-update-slice | bytes 1048580 | tf_op jit(solution)/shard_map/while/body/jit(dynamic_update_index_in_dim)/dynamic_update_slice | solution.py:157
  385.1 8.0 %fusion.179 = (f32[2,512]{1,0:T(2,128)S(1)}, f32[2,512,2048]{2,1,0:T(8,128)}) fusion(pred[512,2048]{1,0:T(8,128)(4,1)S(1)} %iota_compare_fusion.2, bf16[2048,128]{1,0:T(8,128)(2,1)} %get-tuple-element.293, bf16[2048,2,128]{0,2,1:T(8,128)(2,1)} %get-tuple-element.292, s32[]{:T(128)S(6)} %select_n.260), kind=kOutput, calls=%fused_computation.174.clone.1 | convolution fusion | flops 545261568 | bytes 10227716 | tf_op jit(solution)/shard_map/while/body/eval_jaxpr/sub | solution.py:135
  407.4 12.8 %fusion.183 = f32[1,512,2,128]{3,1,2,0:T(8,128)S(1)} fusion(f32[512,2,2048]{2,0,1:T(8,128)} %fusion.178, bf16[2048,128]{1,0:T(8,128)(2,1)S(1)} %copy-done.18, f32[2,512,2048]{2,1,0:T(8,128)} %get-tuple-element.258, f32[2,512]{1,0:T(2,128)S(1)} %get-tuple-element.259), kind=kOutput, calls=%fused_computation.28.clone.1 | convolution fusion | flops 551554048 | bytes 17829888 | tf_op jit(solution)/shard_map/while/body/eval_jaxpr/hst,td->shd/dot_general | solution.py:145
  420.2 19.4 %fusion.180 = f32[2048,128]{1,0:T(8,128)} fusion(f32[512,2,2048]{2,0,1:T(8,128)} %fusion.178, f32[2048,128]{1,0:T(8,128)} %get-tuple-element.274, pred[]{:T(512)S(6)} %compare.38, bf16[2048,2,128]{0,2,1:T(8,128)(2,1)} %get-tuple-element.292, s32[]{:T(128)S(6)} %select_n.260, f32[2,512,2048]{2,1,0:T(8,128)} %get-tuple-element.258, ...), kind=kOutput, calls=%fused_computation.24.clone.1 | convolution fusion | flops 552078336 | bytes 35921924 | tf_op jit(solution)/shard_map/while/body/eval_jaxpr/hst,shd->td/dot_general | solution.py:148
  440.0 11.1 %dynamic_update_slice.14 = f32[4,512,2,128]{1,0,3,2:T(4,128)} dynamic-update-slice(f32[4,512,2,128]{1,0,3,2:T(4,128)} %get-tuple-element.277, f32[1,512,2,128]{1,0,3,2:T(1,128)S(1)} %copy.66, s32[]{:T(128)S(6)} %copy.74, s32[]{:T(128)} %constant.177.clone.1..sunk, s32[]{:T(128)} %constant.177.clone.1..sunk, s32[]{:T(128)} %constant.177.clone.1..sunk) | dynamic-update-slice | bytes 1048580 | tf_op jit(solution)/shard_map/while/body/jit(dynamic_update_index_in_dim)/dynamic_update_slice | solution.py:157
  460.4 11.9 %fusion.87 = bf16[2048,256]{0,1:T(8,128)(2,1)S(1)} fusion(f32[2048,1]{0,1:T(1,128)S(1)} %get-tuple-element.176, f32[2048,255]{0,1:T(8,128)} %get-tuple-element.178, f32[2048,255]{0,1:T(8,128)} %get-tuple-element.177, f32[2048,1]{0,1:T(1,128)S(1)} %get-tuple-element.175, f32[2048,256]{0,1:T(8,128)} %bitcast.183, f32[256]{0:T(256)S(1)} %copy-done.25, ...), kind=kLoop, calls=%fused_computation.95 | loop fusion | flops 5242880 | bytes 7341312 | tf_op jit(solution)/shard_map/convert_element_type | solution.py:175
  490.2 13.5 %fusion.135 = f32[2048,4096]{1,0:T(8,128)} fusion(bf16[2048,32]{0,1:T(8,128)(2,1)S(1)} %fusion.99, bf16[4096,32]{0,1:T(8,128)(2,1)S(1)} %copy-done.12), kind=kOutput, calls=%fused_computation.184 | convolution fusion | flops 536870912 | bytes 33947648 | tf_op jit(solution)/shard_map/sc,dc->sd/dot_general | solution.py:178
  503.8 13.3 %fusion.109 = f32[2048,4096]{1,0:T(8,128)} fusion(bf16[4096,32]{0,1:T(8,128)(2,1)S(1)} %copy-done.14, f32[2,2048,32]{1,2,0:T(8,128)S(1)} %convert_add_fusion.1), kind=kOutput, calls=%fused_computation.144 | convolution fusion | flops 536870912 | bytes 33947648 | tf_op jit(solution)/shard_map/sc,dc->sd/dot_general | solution.py:178
  517.1 28.8 %multiply_convert_fusion = bf16[2048,4096]{1,0:T(8,128)(2,1)} fusion(f32[2048,4096]{1,0:T(8,128)} %fusion.109, f32[2048,4096]{1,0:T(8,128)} %fusion.135, bf16[2048,256]{0,1:T(8,128)(2,1)} %copy-done.8, bf16[4096,256]{1,0:T(8,128)(2,1)S(1)} %copy-done), kind=kOutput, calls=%fused_computation.57 | convolution fusion | flops 4328521728 | bytes 87031808 | tf_op jit(solution)/shard_map/sc,dc->sd/dot_general | solution.py:178
  546.0 14.0 %copy.42 = bf16[2,8,128,4096]{3,2,1,0:T(8,128)(2,1)} copy(bf16[2,8,128,4096]{3,2,0,1:T(8,128)(2,1)} %bitcast.179) | data formatting | bytes 33554432 | tf_op jit(solution)/shard_map/transpose | solution.py:35
  569.5 9.4 %psum.36 = f32[]{:T(128)} all-reduce(f32[]{:T(128)} %psum.35), channel_id=1, replica_groups=mesh['dp_0'=2,'dp_1'=4,'tensor_0'=2,'tensor_1'=4,'tensor_2'=2] {'dp_1'}, use_global_device_ids=true, to_apply=%region_14.15 | all-reduce | flops 1 | bytes 8 | tf_op jit(solution)/shard_map/psum | solution.py:51
  578.9 5.9 psum.37
  585.7 7.2 psum.38
  594.2 9.2 %psum.39 = f32[]{:T(128)} all-reduce(f32[]{:T(128)} %psum.38), channel_id=1, replica_groups=mesh['dp_0'=2,'dp_1'=4,'tensor_0'=2,'tensor_1'=4,'tensor_2'=2] {'tensor_2'}, use_global_device_ids=true, to_apply=%region_17.18 | all-reduce | flops 1 | bytes 8 | tf_op jit(solution)/shard_map/psum | solution.py:51
  611.5 29.4 %all-gather.5.cloned.1.call-done = bf16[4096,320]{0,1:T(8,128)(2,1)} async-done(((bf16[512,320]{0,1:T(8,128)(2,1)}), bf16[4096,320]{0,1:T(8,128)(2,1)}) %all-gather.5.cloned.1.call-update) | async-done | bytes 2621456 | tf_op jit(solution)/shard_map/all_gather | solution.py:61
  650.1 112.2 %reduce-scatter.6.cloned.1.call-done = bf16[1,128,4096]{2,1,0:T(8,128)(2,1)} async-done(((bf16[8,128,4096]{2,1,0:T(8,128)(2,1)}), bf16[1,128,4096]{2,1,0:T(8,128)(2,1)}) %reduce-scatter.6.cloned.1.call-update) | async-done | bytes 1048592 | tf_op jit(solution)/shard_map/reduce_scatter | solution.py:37
  (215 shorter events, 144.7 us)
Async XLA Ops:
  7.2 135.9 %copy-start = (bf16[4096,256]{1,0:T(8,128)(2,1)S(1)}, bf16[4096,256]{1,0:T(8,128)(2,1)}, u32[]{:S(2)}) copy-start(bf16[4096,256]{1,0:T(8,128)(2,1)} %param.14) | copy-start | bytes 6291460
  7.2 117.8 %all-gather.3.cloned.1.call-start = ((), (), s32[]{:S(2)}) async-start(), calls=%async_computation.3 | async-start | bytes 17825792 | tf_op jit(solution)/shard_map/all_gather | solution.py:90
  9.5 115.5 %copy-start.11 = (bf16[4096,32]{0,1:T(8,128)(2,1)S(1)}, bf16[4096,32]{0,1:T(8,128)(2,1)}, u32[]{:S(2)}) copy-start(bf16[4096,32]{0,1:T(8,128)(2,1)} %param.15) | copy-start | bytes 786436
  12.1 547.9 %reduce-scatter.8.cloned.1.call-start = ((), (), s32[]{:S(2)}) async-start(), calls=%async_computation.6 | async-start | bytes 2949120 | tf_op jit(solution)/shard_map/reduce_scatter | solution.py:42
  13.8 122.3 %copy-start.26 = (pred[32]{0:T(512)(128)(4,1)}, pred[32]{0:T(512)(128)(4,1)S(1)}, u32[]{:S(2)}) copy-start(pred[32]{0:T(512)(128)(4,1)S(1)} %fusion.113) | copy-start | bytes 100
  13.8 122.3 %copy-start.28 = (f32[32]{0:T(128)}, f32[32]{0:T(128)S(1)}, u32[]{:S(2)}) copy-start(f32[32]{0:T(128)S(1)} %multiply_power_fusion.1) | copy-start | bytes 388
  13.8 142.0 %copy-start.30 = (pred[256]{0:T(512)(128)(4,1)}, pred[256]{0:T(512)(128)(4,1)S(1)}, u32[]{:S(2)}) copy-start(pred[256]{0:T(512)(128)(4,1)S(1)} %fusion.112) | copy-start | bytes 772
  13.9 142.0 %copy-start.24 = (f32[256]{0:T(256)}, f32[256]{0:T(256)S(1)}, u32[]{:S(2)}) copy-start(f32[256]{0:T(256)S(1)} %multiply_power_fusion) | copy-start | bytes 3076
  13.9 123.5 %copy-start.13 = (bf16[4096,32]{0,1:T(8,128)(2,1)S(1)}, bf16[4096,32]{0,1:T(8,128)(2,1)}, u32[]{:S(2)}) copy-start(bf16[4096,32]{0,1:T(8,128)(2,1)} %param.16) | copy-start | bytes 786436
  125.0 12.4 %copy-start.1 = (bf16[2048,4096]{1,0:T(8,128)(2,1)S(1)}, bf16[2048,4096]{1,0:T(8,128)(2,1)}, u32[]{:S(2)}) copy-start(bf16[2048,4096]{1,0:T(8,128)(2,1)} %all-gather.3.cloned.1.call-done) | copy-start | bytes 50331652
  142.5 13.1 %collective-permute-start = (bf16[2,2048,32]{1,2,0:T(8,128)(2,1)S(1)}, bf16[2,2048,32]{1,2,0:T(8,128)(2,1)S(1)}, u32[]{:S(2)}, u32[]{:S(2)}) collective-permute-start(bf16[2,2048,32]{1,2,0:T(8,128)(2,1)S(1)} %pad_maximum_fusion.3), channel_id=1, source_target_pairs={{0,1},{1,0},{2,3},{3,2},{4,5},{5,4},{6,7},{7,6},{8,9},{9,8},{10,11... | collective-permute-start | bytes 786440 | tf_op jit(solution)/shard_map/ppermute | solution.py:22
  155.8 13.3 %collective-permute-start.1 = (bf16[2,2048,64]{1,2,0:T(8,128)(2,1)S(1)}, bf16[2,2048,64]{1,2,0:T(8,128)(2,1)S(1)}, u32[]{:S(2)}, u32[]{:S(2)}) collective-permute-start(bf16[2,2048,64]{1,2,0:T(8,128)(2,1)S(1)} %maximum_select_fusion.1), channel_id=1, source_target_pairs={{0,2},{1,3},{2,0},{3,1},{4,6},{5,7},{6,4},{7,5},{8,10},{9,11},{10,... | collective-permute-start | bytes 1572872 | tf_op jit(solution)/shard_map/ppermute | solution.py:22
  183.3 5.9 copy-start.7
  183.3 5.9 copy-start.15
  183.3 6.7 copy-start.32
  253.2 6.7 copy-start.32
  323.1 6.7 copy-start.32
  393.1 6.7 copy-start.32
  459.6 15.2 %copy-start.2 = (bf16[2048,4096]{1,0:T(8,128)(2,1)S(1)}, bf16[2048,4096]{1,0:T(8,128)(2,1)}, u32[]{:S(2)}) copy-start(bf16[2048,4096]{1,0:T(8,128)(2,1)} %all-gather.3.cloned.1.call-done) | copy-start | bytes 50331652
  460.0 12.4 %collective-permute-start.2 = (bf16[2,2048,64]{1,2,0:T(8,128)(2,1)S(1)}, bf16[2,2048,64]{1,2,0:T(8,128)(2,1)S(1)}, u32[]{:S(2)}, u32[]{:S(2)}) collective-permute-start(bf16[2,2048,64]{1,2,0:T(8,128)(2,1)S(1)} %select_convert_fusion), channel_id=1, source_target_pairs={{0,2},{1,3},{2,0},{3,1},{4,6},{5,7},{6,4},{7,5},{8,10},{9,11},{10,... | collective-permute-start | bytes 1572872 | tf_op jit(solution)/shard_map/ppermute | solution.py:22
  472.3 7.1 copy-start.8
  472.7 6.8 collective-permute-start.3
  489.3 14.5 %copy-start.14 = (bf16[4096,32]{0,1:T(8,128)(2,1)S(1)}, bf16[4096,32]{0,1:T(8,128)(2,1)}, u32[]{:S(2)}) copy-start(bf16[4096,32]{0,1:T(8,128)(2,1)} %param.16) | copy-start | bytes 786436
  489.3 118.1 %reduce-scatter.4.cloned.1.call-start = ((), (), s32[]{:S(2)}) async-start(), calls=%async_computation.4 | async-start | bytes 25165824 | tf_op jit(solution)/shard_map/reduce_scatter | solution.py:36
  559.9 44.1 %copy-start.20 = (f32[512,32]{0,1:T(8,128)S(1)}, f32[512,32]{0,1:T(8,128)}, u32[]{:S(2)}) copy-start(f32[512,32]{0,1:T(8,128)} %param.18) | copy-start | bytes 196612
  560.0 44.1 %copy-start.21 = (f32[512,32]{0,1:T(8,128)S(1)}, f32[512,32]{0,1:T(8,128)}, u32[]{:S(2)}) copy-start(f32[512,32]{0,1:T(8,128)} %param.19) | copy-start | bytes 196612
  560.0 80.9 %all-gather.5.cloned.1.call-start = ((), (), s32[]{:S(2)}) async-start(), calls=%async_computation.7 | async-start | bytes 2949120 | tf_op jit(solution)/shard_map/all_gather | solution.py:61
  560.1 45.5 %copy-start.10 = (bf16[512,320]{0,1:T(8,128)(2,1)S(1)}, bf16[512,320]{0,1:T(8,128)(2,1)}, u32[]{:S(2)}) copy-start(bf16[512,320]{0,1:T(8,128)(2,1)} %reduce-scatter.8.cloned.1.call-done) | copy-start | bytes 983044
  607.4 154.9 %reduce-scatter.6.cloned.1.call-start = ((), (), s32[]{:S(2)}) async-start(), calls=%async_computation.5 | async-start | bytes 9437184 | tf_op jit(solution)/shard_map/reduce_scatter | solution.py:37
  644.1 118.2 %copy-start.6 = (bf16[1,128,4096]{2,1,0:T(8,128)(2,1)S(1)}, bf16[1,128,4096]{2,1,0:T(8,128)(2,1)}, u32[]{:S(2)}) copy-start(bf16[1,128,4096]{2,1,0:T(8,128)(2,1)} %param.11) | copy-start | bytes 3145732
  644.1 118.2 %copy-start.19 = (f32[4096]{0:T(1024)S(1)}, f32[4096]{0:T(1024)}, u32[]{:S(2)}) copy-start(f32[4096]{0:T(1024)} %param.13) | copy-start | bytes 49156
  644.1 118.2 %copy-start.23 = (f32[128]{0:T(128)S(1)}, f32[128]{0:T(128)}, u32[]{:S(2)}) copy-start(f32[128]{0:T(128)} %copy-done.22) | copy-start | bytes 1540
  (28 other events, 89.9 us)
Sparse Core Ops, SparseCore 0:
  12.3 112.7 all-gather.2
  489.4 37.3 reduce-scatter.7
  560.1 26.7 reduce-scatter.3
  607.5 33.3 all-gather.4
  645.1 117.1 reduce-scatter.5
where the time goes:
time: 781 us; the launch traced here: 772 us
  matrix products  299 us (38%)
  waiting for transfers between devices  256 us (33%)
  local copies, waits for them, and re-layouts  105 us (13%)
  other arithmetic  47.3 us (6%)
  blocking collectives  36.1 us (5%)
  between operations  17.2 us (2%)
  loops' own time  8.27 us (1%)
    reduce_scatter x1, waiting for transfers between devices, summed_rows(): return lax.psum_scatter(pieces, chips, scatter_dimension=0, tiled=True)[0]  112 us
    all_gather x1, waiting for transfers between devices, per_device(): normed_all = lax.all_gather(normed, TENSOR, axis=0, tiled=True)  111 us
    dot_general x4, matrix products, attend(): jnp.einsum('hst,shd->td', grad_low, query_rows, preferred_element_type=jn...  77.6 us
    dot_general x3, matrix products, product(): jnp.einsum('sc,dc->sd', grad, weight, preferred_element_type=jnp.float32)  55.7 us
    dot_general x4, matrix products, attend(): jnp.einsum('hst,td->shd', grad_low, key_head, preferred_element_type=jnp....  51.1 us
    dynamic_update_slice x12, local copies, waits for them, and re-layouts, per_device(): lax.scan(attend, (empty, empty), starts)  49.8 us
    psum x5, blocking collectives, one_axis_at_a_time(): shard = lax.psum(shard, axis)  36.1 us
    sub x4, matrix products, attend(): attention = jax.nn.softmax(jnp.where(causal[None], scores, -1e+30), axis=2)  32 us
  transfers between devices with their start and end apart: 9, of which 5 were waited for; matrix products, arithmetic and copies ran while one was open for 17% of the time, Pallas kernels for 0%

commit v1 on v0

--- a/solution.py
+++ b/solution.py
@@ -16,6 +16,13 @@
 stat_eps = 1e-06
 learn_rate = 0.05
 keep_rate = 0.9
+
+
+def all_by_exchange(x, name, dim):
+    peers = lax.axis_size(name)
+    tiles = jnp.stack([x for _ in range(peers)])
+    tiles = lax.all_to_all(tiles, name, split_axis=0, concat_axis=0)
+    return jnp.concatenate(tiles, axis=dim)
 
 
 def partner_2(shard, axis, distance):
@@ -87,7 +94,7 @@
     reciprocal = lax.rsqrt(jnp.mean(inputs * inputs, axis=1, keepdims=True) + norm_eps)
     unit_rows = inputs * reciprocal
     normed = (unit_rows * gain).astype(jnp.bfloat16)
-    normed_all = lax.all_gather(normed, TENSOR, axis=0, tiled=True)
+    normed_all = all_by_exchange(normed, TENSOR, 0)
     length = normed_all.shape[0]
     query = rotate(
         jnp.dot(normed_all, w_query, preferred_element_type=jnp.float32) * in_scale,

time: 781 us -> 959 us (1.23)
  waiting for transfers between devices: 256 us -> 397 us
  matrix products: 299 us -> 335 us
  local copies, waits for them, and re-layouts: 105 us -> 78.9 us
  starting transfers between devices: 3.25 us -> 18.8 us
    all_to_all x0 -> x1, waiting for transfers between devices: none -> 251 us  [all_by_exchange(): tiles = lax.all_to_all(tiles, name, split_axis=0, concat_axis=0)]
    all_gather x1 -> x0, waiting for transfers between devices: 111 us -> none  [per_device(): normed_all = lax.all_gather(normed, TENSOR, axis=0, tiled=True)]
    dynamic_update_slice x12 -> x4, local copies, waits for them, and re-layouts: 49.8 us -> 3.9 us  [per_device(): lax.scan(attend, (empty, empty), starts)]
  transfers between devices with their start and end apart: 9 -> 9, of which waited for: 5 -> 4; matrix products, arithmetic and copies ran while one was open for 17% -> 17% of each run, Pallas kernels for 0% -> 0%
where the time goes in v1:
time: 959 us; the launch traced here: 951 us
  waiting for transfers between devices  397 us (41%)
  matrix products  335 us (35%)
  local copies, waits for them, and re-layouts  78.9 us (8%)
  other arithmetic  46.6 us (5%)
  blocking collectives  39.6 us (4%)
  starting transfers between devices  18.8 us (2%)
  between operations  17.4 us (2%)
  loops' own time  17.3 us (2%)
    all_to_all x1, waiting for transfers between devices, all_by_exchange(): tiles = lax.all_to_all(tiles, name, split_axis=0, concat_axis=0)  251 us
    reduce_scatter x1, waiting for transfers between devices, summed_rows(): return lax.psum_scatter(pieces, chips, scatter_dimension=0, tiled=True)[0]  112 us
    dot_general x4, matrix products, attend(): jnp.einsum('hst,shd->td', grad_low, query_rows, preferred_element_type=jn...  77.9 us
    dot_general x3, matrix products, product(): jnp.einsum('sc,dc->sd', grad, weight, preferred_element_type=jnp.float32)  59.6 us
    dot_general x4, matrix products, attend(): jnp.einsum('hst,td->shd', grad_low, key_head, preferred_element_type=jnp....  54.3 us
    psum x5, blocking collectives, one_axis_at_a_time(): shard = lax.psum(shard, axis)  39.6 us
    sub x4, matrix products, attend(): attention = jax.nn.softmax(jnp.where(causal[None], scores, -1e+30), axis=2)  32 us
    all_gather x1, waiting for transfers between devices, in_one_piece(): lax.all_gather(both, axis, axis=dim, tiled=True)  31.7 us
  transfers between devices with their start and end apart: 9, of which 4 were waited for; matrix products, arithmetic and copies ran while one was open for 17% of the time, Pallas kernels for 0%

profile of v1, /device:TPU:1, one launch (start us, length us, event | category | flops | bytes accessed | tf_op | source)
XLA Modules:
  0.0 950.7 jit_solution(13695385576836338748)
XLA Ops:
  16.9 8.6 all-to-all-start
  29.0 250.9 %all-to-all-done = bf16[16,128,4096]{2,1,0:T(8,128)(2,1)} async-done(((bf16[16,128,4096]{2,1,0:T(8,128)(2,1)}), bf16[16,128,4096]{2,1,0:T(8,128)(2,1)}, u32[]{:S(2)}, u32[]{:S(2)}) %all-to-all-start) | async-done | bytes 16777248 | tf_op jit(solution)/shard_map/all_to_all | solution.py:24
  279.9 10.8 %convolution_multiply_fusion.5 = f32[2048,32]{0,1:T(8,128)S(1)} fusion(bf16[2048,4096]{1,0:T(8,128)(2,1)} %bitcast.2, bf16[4096,32]{0,1:T(8,128)(2,1)S(1)} %copy-done.12), kind=kOutput, calls=%fused_computation.78 | convolution fusion | flops 536936448 | bytes 17301504 | tf_op jit(solution)/shard_map/dot_general | solution.py:106
  290.9 10.8 %fusion.72 = bf16[1,2048,32]{1,2,0:T(8,128)(2,1)S(1)} fusion(bf16[2048,4096]{1,0:T(8,128)(2,1)} %bitcast.2, bf16[4096,32]{0,1:T(8,128)(2,1)S(1)} %copy-done.14), kind=kOutput, calls=%fused_computation.80 | convolution fusion | flops 537001984 | bytes 17170432 | tf_op jit(solution)/shard_map/dot_general | solution.py:112
  304.2 9.8 %convolution_multiply_fusion.3 = f32[2048,256]{0,1:T(8,128)} fusion(bf16[2048,4096]{1,0:T(8,128)(2,1)} %bitcast.2, bf16[4096,256]{1,0:T(8,128)(2,1)S(1)} %copy-done), kind=kOutput, calls=%fused_computation.67 | convolution fusion | flops 4295491584 | bytes 20971520 | tf_op jit(solution)/shard_map/dot_general | solution.py:100
  323.3 10.3 %fusion.89 = bf16[2048,256]{0,1:T(8,128)(2,1)} fusion(f32[2048,1]{0,1:T(1,128)S(1)} %get-tuple-element.180, f32[2048,255]{0,1:T(8,128)S(1)} %get-tuple-element.182, f32[2048,255]{0,1:T(8,128)S(1)} %get-tuple-element.181, f32[2048,1]{0,1:T(1,128)S(1)} %get-tuple-element.179, f32[2048,256]{0,1:T(8,128)S(1)} %copy-done.2, f32[256]{0:T(256)S(1)} %multiply_power_fusion.1, ...), kind=kLoop, calls=%fused_computation.98 | loop fusion | flops 4718592 | bytes 7341312 | tf_op jit(solution)/shard_map/convert_element_type | solution.py:104
  338.0 247.3 %while.17 = (s32[]{:T(128)}, f32[2048,128]{1,0:T(8,128)}, f32[2048,128]{1,0:T(8,128)}, bf16[4,512,2,128]{3,2,1,0:T(2,128)(2,1)}, f32[4,512,2,128]{3,1,2,0:T(8,12...) while((s32[]{:T(128)}, f32[2048,128]{1,0:T(8,128)}, ...), condition=%wide.region_5.6_spmd.clone, body=%wide.region_1.5_spmd.clone.sunk | while | flops 3269599744 | bytes 153387344 | solution.py:164
  341.4 8.0 fusion.200
  363.2 19.4 %fusion.201 = f32[2048,128]{1,0:T(8,128)} fusion(f32[512,2,2048]{2,0,1:T(8,128)} %fusion.199, f32[2048,128]{1,0:T(8,128)} %get-tuple-element.280, pred[]{:T(512)S(6)} %compare.41, bf16[2048,2,128]{0,2,1:T(8,128)(2,1)} %get-tuple-element.298, s32[]{:T(128)S(6)} %select_n.302, f32[2,512,2048]{2,1,0:T(8,128)} %get-tuple-element.264, ...), kind=kOutput, calls=%fused_computation.24.clone.1 | convolution fusion | flops 552078336 | bytes 35921924 | tf_op jit(solution)/shard_map/while/body/eval_jaxpr/hst,shd->td/dot_general | solution.py:155
  382.6 13.6 %fusion.204 = f32[4,512,2,128]{3,1,2,0:T(8,128)} fusion(f32[4,512,2,128]{3,1,2,0:T(8,128)} %get-tuple-element.283, s32[]{:T(128)S(6)} %copy.75, f32[512,2,2048]{2,0,1:T(8,128)} %fusion.199, bf16[2048,128]{1,0:T(8,128)(2,1)S(1)} %copy-done.18, f32[2,512,2048]{2,1,0:T(8,128)} %get-tuple-element.264, f32[2,512]{1,0:T(2,128)S(1)} %get-tuple-element.265), kind=kOutput, calls=%fused_computation.29.clone.1 | convolution fusion | flops 551554048 | bytes 34611204 | tf_op jit(solution)/shard_map/while/body/eval_jaxpr/hst,td->shd/dot_general | solution.py:152
  399.6 8.0 fusion.200
  422.6 19.5 %fusion.201 = f32[2048,128]{1,0:T(8,128)} fusion(f32[512,2,2048]{2,0,1:T(8,128)} %fusion.199, f32[2048,128]{1,0:T(8,128)} %get-tuple-element.280, pred[]{:T(512)S(6)} %compare.41, bf16[2048,2,128]{0,2,1:T(8,128)(2,1)} %get-tuple-element.298, s32[]{:T(128)S(6)} %select_n.302, f32[2,512,2048]{2,1,0:T(8,128)} %get-tuple-element.264, ...), kind=kOutput, calls=%fused_computation.24.clone.1 | convolution fusion | flops 552078336 | bytes 35921924 | tf_op jit(solution)/shard_map/while/body/eval_jaxpr/hst,shd->td/dot_general | solution.py:155
  442.1 13.6 %fusion.204 = f32[4,512,2,128]{3,1,2,0:T(8,128)} fusion(f32[4,512,2,128]{3,1,2,0:T(8,128)} %get-tuple-element.283, s32[]{:T(128)S(6)} %copy.75, f32[512,2,2048]{2,0,1:T(8,128)} %fusion.199, bf16[2048,128]{1,0:T(8,128)(2,1)S(1)} %copy-done.18, f32[2,512,2048]{2,1,0:T(8,128)} %get-tuple-element.264, f32[2,512]{1,0:T(2,128)S(1)} %get-tuple-element.265), kind=kOutput, calls=%fused_computation.29.clone.1 | convolution fusion | flops 551554048 | bytes 34611204 | tf_op jit(solution)/shard_map/while/body/eval_jaxpr/hst,td->shd/dot_general | solution.py:152
  459.2 8.0 fusion.200
  482.2 19.5 %fusion.201 = f32[2048,128]{1,0:T(8,128)} fusion(f32[512,2,2048]{2,0,1:T(8,128)} %fusion.199, f32[2048,128]{1,0:T(8,128)} %get-tuple-element.280, pred[]{:T(512)S(6)} %compare.41, bf16[2048,2,128]{0,2,1:T(8,128)(2,1)} %get-tuple-element.298, s32[]{:T(128)S(6)} %select_n.302, f32[2,512,2048]{2,1,0:T(8,128)} %get-tuple-element.264, ...), kind=kOutput, calls=%fused_computation.24.clone.1 | convolution fusion | flops 552078336 | bytes 35921924 | tf_op jit(solution)/shard_map/while/body/eval_jaxpr/hst,shd->td/dot_general | solution.py:155
  501.7 13.6 %fusion.204 = f32[4,512,2,128]{3,1,2,0:T(8,128)} fusion(f32[4,512,2,128]{3,1,2,0:T(8,128)} %get-tuple-element.283, s32[]{:T(128)S(6)} %copy.75, f32[512,2,2048]{2,0,1:T(8,128)} %fusion.199, bf16[2048,128]{1,0:T(8,128)(2,1)S(1)} %copy-done.18, f32[2,512,2048]{2,1,0:T(8,128)} %get-tuple-element.264, f32[2,512]{1,0:T(2,128)S(1)} %get-tuple-element.265), kind=kOutput, calls=%fused_computation.29.clone.1 | convolution fusion | flops 551554048 | bytes 34611204 | tf_op jit(solution)/shard_map/while/body/eval_jaxpr/hst,td->shd/dot_general | solution.py:152
  518.7 8.0 fusion.200
  541.7 19.5 %fusion.201 = f32[2048,128]{1,0:T(8,128)} fusion(f32[512,2,2048]{2,0,1:T(8,128)} %fusion.199, f32[2048,128]{1,0:T(8,128)} %get-tuple-element.280, pred[]{:T(512)S(6)} %compare.41, bf16[2048,2,128]{0,2,1:T(8,128)(2,1)} %get-tuple-element.298, s32[]{:T(128)S(6)} %select_n.302, f32[2,512,2048]{2,1,0:T(8,128)} %get-tuple-element.264, ...), kind=kOutput, calls=%fused_computation.24.clone.1 | convolution fusion | flops 552078336 | bytes 35921924 | tf_op jit(solution)/shard_map/while/body/eval_jaxpr/hst,shd->td/dot_general | solution.py:155
  561.2 13.6 %fusion.204 = f32[4,512,2,128]{3,1,2,0:T(8,128)} fusion(f32[4,512,2,128]{3,1,2,0:T(8,128)} %get-tuple-element.283, s32[]{:T(128)S(6)} %copy.75, f32[512,2,2048]{2,0,1:T(8,128)} %fusion.199, bf16[2048,128]{1,0:T(8,128)(2,1)S(1)} %copy-done.18, f32[2,512,2048]{2,1,0:T(8,128)} %get-tuple-element.264, f32[2,512]{1,0:T(2,128)S(1)} %get-tuple-element.265), kind=kOutput, calls=%fused_computation.29.clone.1 | convolution fusion | flops 551554048 | bytes 34611204 | tf_op jit(solution)/shard_map/while/body/eval_jaxpr/hst,td->shd/dot_general | solution.py:152
  615.3 9.8 %fusion.83 = bf16[4,512,2,128]{3,1,2,0:T(8,128)(2,1)S(1)} fusion(f32[4,512,2,128]{3,1,2,0:T(8,128)} %get-tuple-element.69, f32[4,512,2,128]{3,1,2,0:T(8,128)} %copy.47, f32[4,512,2,128]{3,1,2,0:T(8,128)} %copy.48, f32[2,128]{1,0:T(2,128)S(1)} %copy-done.33, f32[4,512]{1,0:T(4,128)S(1)} %copy-done.22, pred[2,128]{1,0:T(4,128)(4,1)S(1)} %copy-done.34), kind=kLoop, calls=%fused_computation.91 | loop fusion | flops 3670016 | bytes 7349504 | tf_op jit(solution)/shard_map/convert_element_type | solution.py:182
  628.1 10.6 %fusion.64 = bf16[4096,256]{0,1:T(8,128)(2,1)S(1)} fusion(bf16[2048,4096]{1,0:T(8,128)(2,1)} %bitcast.2, bf16[256,8,2,128]{3,2,1,0:T(2,128)(2,1)S(1)} %bitcast.210), kind=kOutput, calls=%fused_computation.60 | convolution fusion | flops 4297064448 | bytes 19922944 | tf_op jit(solution)/shard_map/sd,sc->dc/dot_general | solution.py:200
  638.9 8.8 fusion.66
  648.4 7.8 fusion.65
  658.9 13.6 %fusion.130 = f32[2048,4096]{1,0:T(8,128)} fusion(bf16[4096,32]{0,1:T(8,128)(2,1)S(1)} %copy-done.15, f32[2,2048,32]{1,2,0:T(8,128)S(1)} %convert_add_fusion.1), kind=kOutput, calls=%fused_computation.168 | convolution fusion | flops 536870912 | bytes 33947648 | tf_op jit(solution)/shard_map/sc,dc->sd/dot_general | solution.py:185
  672.5 13.9 %fusion.114 = f32[2048,4096]{1,0:T(8,128)} fusion(bf16[4096,32]{0,1:T(8,128)(2,1)S(1)} %copy-done.13, f32[2048,1]{0,1:T(1,128)S(1)} %get-tuple-element.189, f32[2048,31]{0,1:T(8,128)S(1)} %copy-done.16, f32[2048,31]{0,1:T(8,128)S(1)} %get-tuple-element.193, f32[2048,1]{0,1:T(1,128)S(1)} %get-tuple-element.188, f32[32]{0:T(128)S(1)} %copy-done.26, ...), kind=kOutput, calls=%fused_computation.149 | convolution fusion | flops 537526272 | bytes 34620416 | tf_op jit(solution)/shard_map/sc,dc->sd/dot_general | solution.py:185
  686.4 32.2 %multiply_convert_fusion = bf16[2048,4096]{1,0:T(8,128)(2,1)} fusion(f32[2048,4096]{1,0:T(8,128)} %fusion.130, f32[2048,4096]{1,0:T(8,128)} %fusion.114, bf16[4096,256]{1,0:T(8,128)(2,1)S(1)} %copy-done, f32[2048,256]{0,1:T(8,128)} %get-tuple-element.199, f32[2048,256]{0,1:T(8,128)} %get-tuple-element.200, f32[2048,256]{0,1:T(8,128)} %bitcast.205, ...), kind=kOutput, calls=%fused_computation.58 | convolution fusion | flops 4332191744 | bytes 92275968 | tf_op jit(solution)/shard_map/sc,dc->sd/dot_general | solution.py:185
  718.5 14.0 %copy.44 = bf16[2,8,128,4096]{3,2,1,0:T(8,128)(2,1)} copy(bf16[2,8,128,4096]{3,2,0,1:T(8,128)(2,1)} %bitcast.201) | data formatting | bytes 33554432 | tf_op jit(solution)/shard_map/transpose | solution.py:42
  742.0 10.3 %psum.36 = f32[]{:T(128)} all-reduce(f32[]{:T(128)} %psum.35), channel_id=1, replica_groups=mesh['dp_0'=2,'dp_1'=4,'tensor_0'=2,'tensor_1'=4,'tensor_2'=2] {'dp_1'}, use_global_device_ids=true, to_apply=%region_14.15 | all-reduce | flops 1 | bytes 8 | tf_op jit(solution)/shard_map/psum | solution.py:58
  759.1 10.2 %psum.38 = f32[]{:T(128)} all-reduce(f32[]{:T(128)} %psum.37), channel_id=1, replica_groups=mesh['dp_0'=2,'dp_1'=4,'tensor_0'=2,'tensor_1'=4,'tensor_2'=2] {'tensor_1'}, use_global_device_ids=true, to_apply=%region_16.17 | all-reduce | flops 1 | bytes 8 | tf_op jit(solution)/shard_map/psum | solution.py:58
  770.5 8.9 psum.39
  787.6 31.7 %all-gather.2.cloned.1.call-done = bf16[4096,320]{0,1:T(8,128)(2,1)} async-done(((bf16[512,320]{0,1:T(8,128)(2,1)}), bf16[4096,320]{0,1:T(8,128)(2,1)}) %all-gather.2.cloned.1.call-update) | async-done | bytes 2621456 | tf_op jit(solution)/shard_map/all_gather | solution.py:68
  828.5 111.8 %reduce-scatter.6.cloned.1.call-done = bf16[1,128,4096]{2,1,0:T(8,128)(2,1)} async-done(((bf16[8,128,4096]{2,1,0:T(8,128)(2,1)}), bf16[1,128,4096]{2,1,0:T(8,128)(2,1)}) %reduce-scatter.6.cloned.1.call-update) | async-done | bytes 1048592 | tf_op jit(solution)/shard_map/reduce_scatter | solution.py:44
  (210 shorter events, 167.1 us)
Async XLA Ops:
  7.2 297.1 %copy-start = (bf16[4096,256]{1,0:T(8,128)(2,1)S(1)}, bf16[4096,256]{1,0:T(8,128)(2,1)}, u32[]{:S(2)}) copy-start(bf16[4096,256]{1,0:T(8,128)(2,1)} %param.14) | copy-start | bytes 6291460
  16.9 263.0 %all-to-all-start = ((bf16[16,128,4096]{2,1,0:T(8,128)(2,1)}), bf16[16,128,4096]{2,1,0:T(8,128)(2,1)}, u32[]{:S(2)}, u32[]{:S(2)}) async-start(bf16[16,128,4096]{2,1,0:T(8,128)(2,1)} %stack.20), calls=%async_computation | async-start | bytes 33554432 | tf_op jit(solution)/shard_map/all_to_all | solution.py:24
  25.5 254.4 %copy-start.12 = (bf16[4096,32]{0,1:T(8,128)(2,1)S(1)}, bf16[4096,32]{0,1:T(8,128)(2,1)}, u32[]{:S(2)}) copy-start(bf16[4096,32]{0,1:T(8,128)(2,1)} %param.15) | copy-start | bytes 786436
  25.5 707.1 %reduce-scatter.8.cloned.1.call-start = ((), (), s32[]{:S(2)}) async-start(), calls=%async_computation.6 | async-start | bytes 2949120 | tf_op jit(solution)/shard_map/reduce_scatter | solution.py:49
  27.1 274.5 %copy-start.23 = (pred[32]{0:T(512)(128)(4,1)}, pred[32]{0:T(512)(128)(4,1)S(1)}, u32[]{:S(2)}) copy-start(pred[32]{0:T(512)(128)(4,1)S(1)} %fusion.136) | copy-start | bytes 100
  27.2 274.5 %copy-start.25 = (f32[32]{0:T(128)}, f32[32]{0:T(128)S(1)}, u32[]{:S(2)}) copy-start(f32[32]{0:T(128)S(1)} %multiply_power_fusion.2) | copy-start | bytes 388
  27.2 296.1 %copy-start.29 = (pred[256]{0:T(512)(128)(4,1)}, pred[256]{0:T(512)(128)(4,1)S(1)}, u32[]{:S(2)}) copy-start(pred[256]{0:T(512)(128)(4,1)S(1)} %fusion.133) | copy-start | bytes 772
  27.8 295.5 %copy-start.27 = (f32[256]{0:T(256)}, f32[256]{0:T(256)S(1)}, u32[]{:S(2)}) copy-start(f32[256]{0:T(256)S(1)} %multiply_power_fusion.1) | copy-start | bytes 3076
  279.9 10.9 %copy-start.14 = (bf16[4096,32]{0,1:T(8,128)(2,1)S(1)}, bf16[4096,32]{0,1:T(8,128)(2,1)}, u32[]{:S(2)}) copy-start(bf16[4096,32]{0,1:T(8,128)(2,1)} %param.16) | copy-start | bytes 786436
  303.1 13.8 %collective-permute-start = (bf16[2,2048,32]{1,2,0:T(8,128)(2,1)S(1)}, bf16[2,2048,32]{1,2,0:T(8,128)(2,1)S(1)}, u32[]{:S(2)}, u32[]{:S(2)}) collective-permute-start(bf16[2,2048,32]{1,2,0:T(8,128)(2,1)S(1)} %pad_maximum_fusion.4), channel_id=1, source_target_pairs={{0,1},{1,0},{2,3},{3,2},{4,5},{5,4},{6,7},{7,6},{8,9},{9,8},{10,11... | collective-permute-start | bytes 786440 | tf_op jit(solution)/shard_map/ppermute | solution.py:29
  317.0 18.6 %collective-permute-start.1 = (bf16[2,2048,64]{1,2,0:T(8,128)(2,1)S(1)}, bf16[2,2048,64]{1,2,0:T(8,128)(2,1)S(1)}, u32[]{:S(2)}, u32[]{:S(2)}) collective-permute-start(bf16[2,2048,64]{1,2,0:T(8,128)(2,1)S(1)} %maximum_select_fusion.1), channel_id=1, source_target_pairs={{0,2},{1,3},{2,0},{3,1},{4,6},{5,7},{6,4},{7,5},{8,10},{9,11},{10,... | collective-permute-start | bytes 1572872 | tf_op jit(solution)/shard_map/ppermute | solution.py:29
  363.2 19.4 %copy-start.18 = (bf16[2048,128]{1,0:T(8,128)(2,1)S(1)}, bf16[2048,128]{1,0:T(8,128)(2,1)}, u32[]{:S(2)}) copy-start(bf16[2048,128]{1,0:T(8,128)(2,1)} %get-tuple-element.299) | copy-start | bytes 1572868 | tf_op jit(solution)/shard_map/while
  422.6 19.5 %copy-start.18 = (bf16[2048,128]{1,0:T(8,128)(2,1)S(1)}, bf16[2048,128]{1,0:T(8,128)(2,1)}, u32[]{:S(2)}) copy-start(bf16[2048,128]{1,0:T(8,128)(2,1)} %get-tuple-element.299) | copy-start | bytes 1572868 | tf_op jit(solution)/shard_map/while
  482.2 19.5 %copy-start.18 = (bf16[2048,128]{1,0:T(8,128)(2,1)S(1)}, bf16[2048,128]{1,0:T(8,128)(2,1)}, u32[]{:S(2)}) copy-start(bf16[2048,128]{1,0:T(8,128)(2,1)} %get-tuple-element.299) | copy-start | bytes 1572868 | tf_op jit(solution)/shard_map/while
  541.7 19.5 %copy-start.18 = (bf16[2048,128]{1,0:T(8,128)(2,1)S(1)}, bf16[2048,128]{1,0:T(8,128)(2,1)}, u32[]{:S(2)}) copy-start(bf16[2048,128]{1,0:T(8,128)(2,1)} %get-tuple-element.299) | copy-start | bytes 1572868 | tf_op jit(solution)/shard_map/while
  598.1 28.0 %collective-permute-start.2 = (bf16[2,2048,64]{1,2,0:T(8,128)(2,1)S(1)}, bf16[2,2048,64]{1,2,0:T(8,128)(2,1)S(1)}, u32[]{:S(2)}, u32[]{:S(2)}) collective-permute-start(bf16[2,2048,64]{1,2,0:T(8,128)(2,1)S(1)} %select_convert_fusion), channel_id=1, source_target_pairs={{0,2},{1,3},{2,0},{3,1},{4,6},{5,7},{6,4},{7,5},{8,10},{9,11},{10,... | collective-permute-start | bytes 1572872 | tf_op jit(solution)/shard_map/ppermute | solution.py:29
  626.9 11.8 %collective-permute-start.3 = (bf16[2,2048,32]{1,2,0:T(8,128)(2,1)S(1)}, bf16[2,2048,32]{1,2,0:T(8,128)(2,1)S(1)}, u32[]{:S(2)}, u32[]{:S(2)}) collective-permute-start(bf16[2,2048,32]{1,2,0:T(8,128)(2,1)S(1)} %select_convert_fusion.1), channel_id=1, source_target_pairs={{0,1},{1,0},{2,3},{3,2},{4,5},{5,4},{6,7},{7,6},{8,9},{9,8},{10,11... | collective-permute-start | bytes 786440 | tf_op jit(solution)/shard_map/ppermute | solution.py:29
  638.8 9.6 %copy-start.24 = (pred[32]{0:T(512)(128)(4,1)S(1)}, pred[32]{0:T(512)(128)(4,1)}, u32[]{:S(2)}) copy-start(pred[32]{0:T(512)(128)(4,1)} %copy-done.23) | copy-start | bytes 100
  638.9 9.6 %copy-start.26 = (f32[32]{0:T(128)S(1)}, f32[32]{0:T(128)}, u32[]{:S(2)}) copy-start(f32[32]{0:T(128)} %copy-done.25) | copy-start | bytes 388
  658.0 14.5 %copy-start.13 = (bf16[4096,32]{0,1:T(8,128)(2,1)S(1)}, bf16[4096,32]{0,1:T(8,128)(2,1)}, u32[]{:S(2)}) copy-start(bf16[4096,32]{0,1:T(8,128)(2,1)} %param.15) | copy-start | bytes 786436
  658.0 125.6 %reduce-scatter.4.cloned.1.call-start = ((), (), s32[]{:S(2)}) async-start(), calls=%async_computation.4 | async-start | bytes 25165824 | tf_op jit(solution)/shard_map/reduce_scatter | solution.py:43
  658.9 13.6 %copy-start.16 = (f32[2048,31]{0,1:T(8,128)S(1)}, f32[2048,31]{0,1:T(8,128)}, u32[]{:S(2)}) copy-start(f32[2048,31]{0,1:T(8,128)} %get-tuple-element.194) | copy-start | bytes 761860
  672.5 13.9 %copy-start.28 = (f32[256]{0:T(256)S(1)}, f32[256]{0:T(256)}, u32[]{:S(2)}) copy-start(f32[256]{0:T(256)} %copy-done.27) | copy-start | bytes 3076
  672.5 13.9 %copy-start.30 = (pred[256]{0:T(512)(128)(4,1)S(1)}, pred[256]{0:T(512)(128)(4,1)}, u32[]{:S(2)}) copy-start(pred[256]{0:T(512)(128)(4,1)} %copy-done.29) | copy-start | bytes 772
  732.5 47.6 %copy-start.20 = (f32[512,32]{0,1:T(8,128)S(1)}, f32[512,32]{0,1:T(8,128)}, u32[]{:S(2)}) copy-start(f32[512,32]{0,1:T(8,128)} %param.18) | copy-start | bytes 196612
  732.6 47.6 %copy-start.21 = (f32[512,32]{0,1:T(8,128)S(1)}, f32[512,32]{0,1:T(8,128)}, u32[]{:S(2)}) copy-start(f32[512,32]{0,1:T(8,128)} %param.19) | copy-start | bytes 196612
  732.6 86.8 %all-gather.2.cloned.1.call-start = ((), (), s32[]{:S(2)}) async-start(), calls=%async_computation.7 | async-start | bytes 2949120 | tf_op jit(solution)/shard_map/all_gather | solution.py:68
  732.7 47.5 %copy-start.11 = (bf16[512,320]{0,1:T(8,128)(2,1)S(1)}, bf16[512,320]{0,1:T(8,128)(2,1)}, u32[]{:S(2)}) copy-start(bf16[512,320]{0,1:T(8,128)(2,1)} %reduce-scatter.8.cloned.1.call-done) | copy-start | bytes 983044
  783.5 156.8 %reduce-scatter.6.cloned.1.call-start = ((), (), s32[]{:S(2)}) async-start(), calls=%async_computation.5 | async-start | bytes 9437184 | tf_op jit(solution)/shard_map/reduce_scatter | solution.py:44
  822.5 117.8 %copy-start.4 = (bf16[1,128,4096]{2,1,0:T(8,128)(2,1)S(1)}, bf16[1,128,4096]{2,1,0:T(8,128)(2,1)}, u32[]{:S(2)}) copy-start(bf16[1,128,4096]{2,1,0:T(8,128)(2,1)} %param.11) | copy-start | bytes 3145732
  822.5 117.8 %copy-start.19 = (f32[4096]{0:T(1024)S(1)}, f32[4096]{0:T(1024)}, u32[]{:S(2)}) copy-start(f32[4096]{0:T(1024)} %param.13) | copy-start | bytes 49156
  822.5 117.8 %copy-start.32 = (f32[128]{0:T(128)S(1)}, f32[128]{0:T(128)}, u32[]{:S(2)}) copy-start(f32[128]{0:T(128)} %copy-done.31) | copy-start | bytes 1540
  (25 other events, 98.6 us)
Sparse Core Ops, SparseCore 0:
  658.1 42.9 reduce-scatter.7
  732.7 32.2 reduce-scatter.3
  783.7 35.6 all-gather.1
  823.5 116.7 reduce-scatter.5
